TPU v7x, 256 devices: a whole 4x4x8 slice. The times are simulated.
256 devices in a mesh: pipe: 16 (over y, x_lo, core), fsdp: 8 (over z), tp: 2 (over x_hi).
Axes of the slice: x: 4 (x_hi: 2, x_lo: 2; x = x_hi * 2 + x_lo), y: 4, z: 8, core: 2. Of those that a mesh axis runs over, the one named last changes fastest.
Arguments:
- act_in: bfloat16 [16, 2, 8, 128, 4096], P('pipe', None, 'fsdp', None, 'tp'), may hold values from -6 to 6
- gate_q: bfloat16 [16, 2, 8, 128, 4096], P('pipe', None, 'fsdp', None, 'tp'), may hold values from -6 to 6
- gate_k: bfloat16 [16, 2, 8, 128, 4096], P('pipe', None, 'fsdp', None, 'tp'), may hold values from -6 to 6
- grad_in: bfloat16 [16, 8, 128, 4096], P('pipe', 'fsdp', None, 'tp'), may hold values from -6 to 6
- weight: bfloat16 [16, 4096, 4096], P('pipe', 'tp', 'fsdp'), may hold values from -0.09375 to 0.09375
- filters: bfloat16 [16, 128, 256], P('pipe', None, 'tp'), may hold values from -0.5 to 0.5
Outputs:
- grad_out: bfloat16 [16, 2, 8, 128, 4096], P('pipe', None, 'fsdp', None, 'tp')
- filter_grad: float32 [16, 128, 256], P('pipe', 'fsdp', 'tp')
All inputs are finite; a program needn't handle non-finite values.
Results may differ from a plain program's by a relative error of at most 0.0056.
Values may be sent and summed in bfloat16 or wider, within the bound.
No kernel may reach another device: no remote copies, remote signals or barrier semaphores. Data moves between devices by JAX's collectives and lax.ppermute only.
A program may use at most 128 MiB of HBM per device.

v0:
```python
import math
import jax
import jax.numpy as jnp
from jax import lax
from jax.sharding import PartitionSpec as P


def passed_along(value, axis, by):
    peers = lax.axis_size(axis)
    pairs = [(i, i + by) for i in range(peers) if 0 <= i + by < peers]
    return lax.ppermute(value, axis, pairs)


def toeplitz(taps_table, seqlen):
    rows = taps_table.T
    padded = jnp.pad(rows, ((0, 0), (0, 2 * seqlen - rows.shape[1])))
    tiled = jnp.tile(padded, (1, seqlen))
    cut = tiled[:, : seqlen * (2 * seqlen - 1)].reshape(rows.shape[0], seqlen, 2 * seqlen - 1)
    return cut[:, :, :seqlen]


def filter_terms(adjoint, shaped, taps):
    seqlen = adjoint.shape[0]
    groups_loc = adjoint.shape[1]
    flipped = jnp.pad(shaped[::-1], ((0, taps), (0, 0), (0, 0)))
    span = seqlen + taps
    block = math.gcd(groups_loc, 16)
    pieces = []
    for first in range(0, groups_loc, block):
        corr = jnp.einsum(
            "tgc,ugc->gtu",
            adjoint[:, first : first + block],
            flipped[:, first : first + block],
            preferred_element_type=jnp.float32,
        )
        flat = corr.reshape(block, seqlen * span)[:, : seqlen * (span - 1)]
        skewed = flat.reshape(block, seqlen, span - 1)[:, :, seqlen - 1 : seqlen - 1 + taps]
        pieces.append(jnp.sum(skewed, axis=1))
    return jnp.concatenate(pieces, axis=0).T


def body(act_in, gate_q, gate_k, grad_in, weight, filters):
    ticks = act_in.shape[1]
    seqlen = act_in.shape[3]
    width_loc = act_in.shape[4]
    taps = filters.shape[1]
    groups_loc = filters.shape[2]
    per_group = width_loc // groups_loc
    scale = 1.0 / math.sqrt(ticks * lax.axis_size("fsdp") * seqlen * per_group)
    kernel = toeplitz(filters[0], seqlen)
    contract = (((1,), (1,)), ((), ()))
    incoming = grad_in[0, 0]
    outputs = []
    pending = jnp.zeros((taps, groups_loc), jnp.float32)
    for tick in range(ticks):
        if tick > 0:
            incoming = passed_along(outputs[-1], "pipe", -1)
        whole = lax.all_gather(incoming, "tp", axis=1, tiled=True)

        def add_panel(total, piece, start, whole=whole):
            return lax.dot_general(whole, piece, contract, preferred_element_type=jnp.float32)

        deriv = add_panel(
            jnp.zeros((seqlen, width_loc), jnp.float32),
            lax.all_gather(weight[0], "fsdp", axis=1, tiled=True),
            jnp.int32(0),
        )
        adjoint = (
            (gate_q[0, tick, 0] * deriv).astype(jnp.bfloat16).reshape(seqlen, groups_loc, per_group)
        )
        back = jnp.einsum(
            "gtu,ugc->tgc", kernel, adjoint, preferred_element_type=jnp.float32
        ).reshape(seqlen, width_loc)
        result = (incoming + gate_k[0, tick, 0] * back).astype(jnp.bfloat16)
        outputs.append(result)
        shaped = (
            gate_k[0, tick, 0].astype(jnp.float32) * act_in[0, tick, 0].astype(jnp.float32)
        ).astype(jnp.bfloat16)
        term = filter_terms(adjoint, shaped.reshape(seqlen, groups_loc, per_group), taps) * scale
        pending = pending + term
    summed = lax.psum_scatter(pending, "fsdp", scatter_dimension=0, tiled=True)
    grads = jnp.stack(outputs, axis=0)[None, :, None]
    return (grads, summed[None])


def solution(mesh):
    placed = (
        P("pipe", None, "fsdp", None, "tp"),
        P("pipe", None, "fsdp", None, "tp"),
        P("pipe", None, "fsdp", None, "tp"),
        P("pipe", "fsdp", None, "tp"),
        P("pipe", "tp", "fsdp"),
        P("pipe", None, "tp"),
    )
    return jax.shard_map(
        body,
        mesh=mesh,
        in_specs=placed,
        out_specs=(P("pipe", None, "fsdp", None, "tp"), P("pipe", "fsdp", "tp")),
        check_vma=False,
    )
```

profile of v0, /device:TPU:2, one launch (start us, length us, event | category | flops | bytes accessed | tf_op | source)
XLA Modules:
  0.0 514.4 jit_solution(2104143820232488051)
XLA Ops:
  8.9 3.8 tile.4
  12.7 12.3 %copy.61 = bf16[16,8,128,256]{3,1,2,0:T(8,128)(2,1)} copy(bf16[16,8,128,256]{3,2,1,0:T(8,128)(2,1)} %bitcast.136) | data formatting | bytes 16777216
  25.0 7.4 %slice.290 = bf16[128,32640]{1,0:T(8,128)(2,1)} slice(bf16[128,32768]{1,0:T(8,128)(2,1)} %bitcast.137), slice={[0:128], [0:32640]} | slice | bytes 16711680 | tf_op jit(solution)/shard_map/slice | solution.py:18
  32.4 29.8 %reshape.184 = bf16[128,128,255]{2,1,0:T(8,128)(2,1)} reshape(bf16[128,32640]{1,0:T(8,128)(2,1)} %slice.290) | data formatting | bytes 16711680 | tf_op jit(solution)/shard_map/reshape | solution.py:18
  64.0 150.7 %all-gather.10.cloned.1.call-done = bf16[1,2048,4096]{2,1,0:T(8,128)(2,1)} async-done(((bf16[1,2048,512]{2,1,0:T(8,128)(2,1)}), bf16[1,2048,4096]{2,1,0:T(8,128)(2,1)}) %all-gather.10.cloned.1.call-update) | async-done | bytes 16777232 | tf_op jit(solution)/shard_map/all_gather | solution.py:65
  214.7 11.8 %fusion.17 = bf16[128,2048]{1,0:T(8,128)(2,1)S(1)} fusion(bf16[1,2048,4096]{2,1,0:T(8,128)(2,1)} %all-gather.10.cloned.1.call-done, bf16[1,1,128,4096]{3,2,1,0:T(8,128)(2,1)} %all-gather.8.cloned.1.call-done, bf16[1,2,1,128,2048]{4,3,2,1,0:T(8,128)(2,1)S(1)} %copy-done.9), kind=kOutput, calls=%fused_computation.11 | convolution fusion | flops 2148270080 | bytes 18874368 | tf_op jit(solution)/shard_map/dot_general | solution.py:61
  226.8 1.7 fusion.33
  233.5 1.8 fusion.37
  236.9 2.3 fusion.6
  240.5 2.6 fusion.23
  243.1 2.1 collective-permute-start
  247.9 6.2 %reshape.190 = f32[16,128,255]{2,1,0:T(8,128)} reshape(f32[16,32640]{1,0:T(8,128)} %slice.292) | data formatting | bytes 4177920 | tf_op jit(solution)/shard_map/reshape | solution.py:37
  254.1 1.9 slice_reduce_fusion.15
  256.1 2.8 copy.63
  260.4 6.1 %reshape.192 = f32[16,128,255]{2,1,0:T(8,128)} reshape(f32[16,32640]{1,0:T(8,128)} %slice.294) | data formatting | bytes 4177920 | tf_op jit(solution)/shard_map/reshape | solution.py:37
  266.5 1.9 slice_reduce_fusion.14
  268.5 2.8 copy.64
  272.7 6.1 %reshape.194 = f32[16,128,255]{2,1,0:T(8,128)} reshape(f32[16,32640]{1,0:T(8,128)} %slice.296) | data formatting | bytes 4177920 | tf_op jit(solution)/shard_map/reshape | solution.py:37
  278.9 1.9 slice_reduce_fusion.13
  280.8 3.2 copy.65
  285.5 6.1 %reshape.196 = f32[16,128,255]{2,1,0:T(8,128)} reshape(f32[16,32640]{1,0:T(8,128)} %slice.298) | data formatting | bytes 4177920 | tf_op jit(solution)/shard_map/reshape | solution.py:37
  291.6 1.9 slice_reduce_fusion.12
  293.5 2.8 copy.66
  297.8 6.3 %reshape.198 = f32[16,128,255]{2,1,0:T(8,128)} reshape(f32[16,32640]{1,0:T(8,128)} %slice.300) | data formatting | bytes 4177920 | tf_op jit(solution)/shard_map/reshape | solution.py:37
  304.0 1.9 slice_reduce_fusion.11
  306.0 2.8 copy.67
  310.3 6.1 %reshape.200 = f32[16,128,255]{2,1,0:T(8,128)} reshape(f32[16,32640]{1,0:T(8,128)} %slice.302) | data formatting | bytes 4177920 | tf_op jit(solution)/shard_map/reshape | solution.py:37
  316.5 1.9 slice_reduce_fusion.10
  318.5 1.7 fusion.39
  322.1 2.8 copy.68
  326.3 6.2 %reshape.202 = f32[16,128,255]{2,1,0:T(8,128)} reshape(f32[16,32640]{1,0:T(8,128)} %slice.304) | data formatting | bytes 4177920 | tf_op jit(solution)/shard_map/reshape | solution.py:37
  332.5 3.0 copy.69
  336.9 6.1 %reshape.204 = f32[16,128,255]{2,1,0:T(8,128)} reshape(f32[16,32640]{1,0:T(8,128)} %slice.306) | data formatting | bytes 4177920 | tf_op jit(solution)/shard_map/reshape | solution.py:37
  344.4 2.0 slice_reduce_fusion.9
  346.4 1.9 slice_reduce_fusion.8
  349.5 12.0 %fusion.14 = bf16[128,2048]{1,0:T(8,128)(2,1)S(1)} fusion(bf16[128,4096]{1,0:T(8,128)(2,1)} %all-gather.6.cloned.1.call-done, bf16[1,2048,4096]{2,1,0:T(8,128)(2,1)} %all-gather.10.cloned.1.call-done, bf16[1,2,1,128,2048]{4,3,2,1,0:T(8,128)(2,1)} %param.7), kind=kOutput, calls=%fused_computation.10 | convolution fusion | flops 2148270080 | bytes 18874368 | tf_op jit(solution)/shard_map/dot_general | solution.py:61
  363.7 1.7 fusion.43
  365.4 1.7 fusion.44
  368.8 1.7 fusion.46
  370.5 1.7 fusion.47
  372.6 3.3 fusion.4
  378.6 6.2 %reshape.206 = f32[16,128,255]{2,1,0:T(8,128)} reshape(f32[16,32640]{1,0:T(8,128)} %slice.308) | data formatting | bytes 4177920 | tf_op jit(solution)/shard_map/reshape | solution.py:37
  384.8 1.9 slice_reduce_fusion.7
  386.8 2.8 copy.71
  391.1 6.1 %reshape.208 = f32[16,128,255]{2,1,0:T(8,128)} reshape(f32[16,32640]{1,0:T(8,128)} %slice.310) | data formatting | bytes 4177920 | tf_op jit(solution)/shard_map/reshape | solution.py:37
  397.2 1.9 slice_reduce_fusion.6
  399.2 3.2 copy.72
  403.8 6.2 %reshape.210 = f32[16,128,255]{2,1,0:T(8,128)} reshape(f32[16,32640]{1,0:T(8,128)} %slice.312) | data formatting | bytes 4177920 | tf_op jit(solution)/shard_map/reshape | solution.py:37
  410.0 1.9 slice_reduce_fusion.5
  411.9 2.8 copy.73
  416.2 6.2 %reshape.212 = f32[16,128,255]{2,1,0:T(8,128)} reshape(f32[16,32640]{1,0:T(8,128)} %slice.314) | data formatting | bytes 4177920 | tf_op jit(solution)/shard_map/reshape | solution.py:37
  422.4 1.9 slice_reduce_fusion.4
  424.3 2.8 copy.74
  428.6 6.2 %reshape.214 = f32[16,128,255]{2,1,0:T(8,128)} reshape(f32[16,32640]{1,0:T(8,128)} %slice.316) | data formatting | bytes 4177920 | tf_op jit(solution)/shard_map/reshape | solution.py:37
  434.8 1.9 slice_reduce_fusion.3
  436.7 3.0 copy.75
  441.1 6.2 %reshape.216 = f32[16,128,255]{2,1,0:T(8,128)} reshape(f32[16,32640]{1,0:T(8,128)} %slice.318) | data formatting | bytes 4177920 | tf_op jit(solution)/shard_map/reshape | solution.py:37
  447.3 1.9 slice_reduce_fusion.2
  449.2 2.8 copy.76
  453.5 6.2 %reshape.218 = f32[16,128,255]{2,1,0:T(8,128)} reshape(f32[16,32640]{1,0:T(8,128)} %slice.320) | data formatting | bytes 4177920 | tf_op jit(solution)/shard_map/reshape | solution.py:37
  459.7 1.9 slice_reduce_fusion.1
  463.0 4.6 reshape.220
  467.6 2.0 slice_reduce_fusion
  473.2 32.9 %reduce-scatter.4.cloned.1.call-done = f32[16,128]{1,0:T(8,128)} async-done(((f32[128,128]{1,0:T(8,128)}), f32[16,128]{1,0:T(8,128)}) %reduce-scatter.4.cloned.1.call-update) | async-done | bytes 8208
  (105 shorter events, 50.9 us)
Async XLA Ops:
  7.2 1.5 copy-start.10
  7.2 56.8 %all-gather.8.cloned.1.call-start = ((), (), s32[]{:S(2)}) async-start(), calls=%async_computation.2 | async-start | bytes 1572864 | tf_op jit(solution)/shard_map/all_gather | solution.py:58
  7.9 206.8 %all-gather.10.cloned.1.call-start = ((), (), s32[]{:S(2)}) async-start(), calls=%async_computation.3 | async-start | bytes 18874368 | tf_op jit(solution)/shard_map/all_gather | solution.py:65
  8.7 340.8 %all-gather.6.cloned.1.call-start = ((), (), s32[]{:S(2)}) async-start(), calls=%async_computation.1 | async-start | bytes 1572864 | tf_op jit(solution)/shard_map/all_gather | solution.py:58
  32.4 29.8 %copy-start.1 = (bf16[1,2,1,128,2048]{4,3,2,1,0:T(8,128)(2,1)S(1)}, bf16[1,2,1,128,2048]{4,3,2,1,0:T(8,128)(2,1)}, u32[]{:S(2)}) copy-start(bf16[1,2,1,128,2048]{4,3,2,1,0:T(8,128)(2,1)} %param.8) | copy-start | bytes 3145732
  32.4 29.8 %copy-start.8 = (bf16[1,2,1,128,2048]{4,3,2,1,0:T(8,128)(2,1)S(1)}, bf16[1,2,1,128,2048]{4,3,2,1,0:T(8,128)(2,1)}, u32[]{:S(2)}) copy-start(bf16[1,2,1,128,2048]{4,3,2,1,0:T(8,128)(2,1)} %param.6) | copy-start | bytes 3145732
  62.6 152.1 %copy-start.9 = (bf16[1,2,1,128,2048]{4,3,2,1,0:T(8,128)(2,1)S(1)}, bf16[1,2,1,128,2048]{4,3,2,1,0:T(8,128)(2,1)}, u32[]{:S(2)}) copy-start(bf16[1,2,1,128,2048]{4,3,2,1,0:T(8,128)(2,1)} %param.7) | copy-start | bytes 3145732
  226.8 10.2 %slice-start = ((s8[8388608]{0:T(1024)(128)(4,1)}), s8[4194304]{0:T(1024)(128)(4,1)S(1)}, s32[]{:S(2)}) async-start(s8[8388608]{0:T(1024)(128)(4,1)} %bitcast.132), calls=%async_computation.5 | async-start | bytes 8388608
  231.8 5.1 slice-start.1
  239.2 1.3 copy-start.4
  240.5 4.7 copy-start
  243.1 78.7 %collective-permute-start = (bf16[128,2048]{1,0:T(8,128)(2,1)}, bf16[128,2048]{1,0:T(8,128)(2,1)}, u32[]{:S(2)}, u32[]{:S(2)}) collective-permute-start(bf16[128,2048]{1,0:T(8,128)(2,1)} %fusion.23), channel_id=1, source_target_pairs={{16,0},{32,16},{48,32},{64,48},{80,64},{96,80},{112,96},{128,112},... | collective-permute-start | bytes 1572872 | tf_op jit(solution)/shard_map/ppermute | solution.py:11
  321.8 184.3 %reduce-scatter.4.cloned.1.call-start = ((), (), s32[]{:S(2)}) async-start(), calls=%async_computation.4 | async-start | bytes 73728
  343.1 5.3 %copy-start.2 = (bf16[1,2,1,128,2048]{4,3,2,1,0:T(8,128)(2,1)S(1)}, bf16[1,2,1,128,2048]{4,3,2,1,0:T(8,128)(2,1)}, u32[]{:S(2)}) copy-start(bf16[1,2,1,128,2048]{4,3,2,1,0:T(8,128)(2,1)} %param.8) | copy-start | bytes 3145732
  344.4 4.0 copy-start.5
  363.7 8.8 %slice-start.2 = ((s8[8388608]{0:T(1024)(128)(4,1)}), s8[4194304]{0:T(1024)(128)(4,1)S(1)}, s32[]{:S(2)}) async-start(s8[8388608]{0:T(1024)(128)(4,1)} %bitcast.134), calls=%async_computation.7 | async-start | bytes 8388608
  368.8 3.8 slice-start.3
  463.0 7.5 %copy-start.6 = (f32[128,16,128]{2,1,0:T(8,128)S(1)}, f32[128,16,128]{2,1,0:T(8,128)}, u32[]{:S(2)}) copy-start(f32[128,16,128]{2,1,0:T(8,128)} %fusion.4) | copy-start | bytes 3145732
  467.6 3.2 copy-start.3
  470.8 1.3 copy-start.7
Sparse Core Ops, SparseCore 0:
  9.8 29.9 all-gather.7
  41.6 173.1 all-gather.9
  322.0 26.2 all-gather.5
  470.6 35.5 reduce-scatter.3
where the time goes:
time: 522 us; the launch traced here: 514 us
  local copies, waits for them, and re-layouts  221 us (42%)
  waiting for transfers between devices  185 us (35%)
  matrix products  53.6 us (10%)
  other arithmetic  37.5 us (7%)
  between operations  14.5 us (3%)
    all_gather x1, waiting for transfers between devices, body(): lax.all_gather(weight[0], 'fsdp', axis=1, tiled=True)  151 us
    reshape x16, local copies, waits for them, and re-layouts, filter_terms(): flat.reshape(block, seqlen, span - 1)[:, :, seqlen - 1:seqlen - 1 + taps]  97.1 us
    unnamed x65, local copies, waits for them, and re-layouts  56 us
    unnamed x5, waiting for transfers between devices  34.4 us
    reduce_sum x16, other arithmetic, filter_terms(): pieces.append(jnp.sum(skewed, axis=1))  31.1 us
    reshape x1, local copies, waits for them, and re-layouts, toeplitz(): tiled[:, :seqlen * (2 * seqlen - 1)]  29.8 us
    dot_general x16, matrix products, filter_terms(): jnp.einsum('tgc,ugc->gtu', adjoint[:, first:first + block], flipped[:, fi...  24.3 us
    dot_general x2, matrix products, add_panel(): lax.dot_general(whole, piece, contract, preferred_element_type=jnp.float32)  23.7 us
  transfers between devices with their start and end apart: 5, of which 2 were waited for; matrix products, arithmetic and copies ran while one was open for 31% of the time, Pallas kernels for 0%

commit v1 on v0

--- a/solution.py
+++ b/solution.py
@@ -62,7 +62,9 @@
 
         deriv = add_panel(
             jnp.zeros((seqlen, width_loc), jnp.float32),
-            lax.all_gather(weight[0], "fsdp", axis=1, tiled=True),
+            jnp.concatenate(
+                lax.all_to_all(jnp.stack([weight[0]] * lax.axis_size("fsdp")), "fsdp", 0, 0), axis=1
+            ),
             jnp.int32(0),
         )
         adjoint = (

time: 522 us -> 690 us (1.32)
  waiting for transfers between devices: 185 us -> 343 us
  local copies, waits for them, and re-layouts: 221 us -> 230 us
  starting transfers between devices: 2.45 us -> 11.1 us
    all_to_all x0 -> x1, waiting for transfers between devices: none -> 311 us  [body(): lax.all_to_all(jnp.stack([weight[0]] * lax.axis_size('fsdp')), 'fsdp', 0, 0)]
    all_gather x1 -> x0, waiting for transfers between devices: 151 us -> none  [body(): lax.all_gather(weight[0], 'fsdp', axis=1, tiled=True)]
    another operation x0 -> x2, local copies, waits for them, and re-layouts: none -> 8.91 us  [the longest x1 5.98 us: body(): jnp.stack([weight[0]] * lax.axis_size('fsdp'))]
    all_to_all x0 -> x1, starting transfers between devices: none -> 8.6 us  [body(): lax.all_to_all(jnp.stack([weight[0]] * lax.axis_size('fsdp')), 'fsdp', 0, 0)]
    unnamed x5 -> x4, waiting for transfers between devices: 34.4 us -> 31.6 us
  transfers between devices with their start and end apart: 5 -> 5, of which waited for: 2 -> 2; matrix products, arithmetic and copies ran while one was open for 31% -> 24% of each run, Pallas kernels for 0% -> 0%
where the time goes in v1:
time: 690 us; the launch traced here: 682 us
  waiting for transfers between devices  343 us (50%)
  local copies, waits for them, and re-layouts  230 us (33%)
  matrix products  47 us (7%)
  other arithmetic  37.4 us (5%)
  between operations  14.5 us (2%)
  starting transfers between devices  11.1 us (2%)
    all_to_all x1, waiting for transfers between devices, body(): lax.all_to_all(jnp.stack([weight[0]] * lax.axis_size('fsdp')), 'fsdp', 0, 0)  311 us
    reshape x16, local copies, waits for them, and re-layouts, filter_terms(): flat.reshape(block, seqlen, span - 1)[:, :, seqlen - 1:seqlen - 1 + taps]  97.6 us
    unnamed x65, local copies, waits for them, and re-layouts  55.3 us
    unnamed x4, waiting for transfers between devices  31.6 us
    reduce_sum x16, other arithmetic, filter_terms(): pieces.append(jnp.sum(skewed, axis=1))  31.1 us
    reshape x1, local copies, waits for them, and re-layouts, toeplitz(): tiled[:, :seqlen * (2 * seqlen - 1)]  29.7 us
    dot_general x16, matrix products, filter_terms(): jnp.einsum('tgc,ugc->gtu', adjoint[:, first:first + block], flipped[:, fi...  24.5 us
    slice x16, local copies, waits for them, and re-layouts, filter_terms(): flat = corr.reshape(block, seqlen * span)[:, :seqlen * (span - 1)]  22.2 us
  transfers between devices with their start and end apart: 5, of which 2 were waited for; matrix products, arithmetic and copies ran while one was open for 24% of the time, Pallas kernels for 0%

profile of v1, /device:TPU:2, one launch (start us, length us, event | category | flops | bytes accessed | tf_op | source)
XLA Modules:
  0.0 682.4 jit_solution(12074562438394179487)
XLA Ops:
  7.2 2.9 copy.51
  10.1 6.0 stack.11
  16.1 8.6 %all-to-all-start = ((bf16[8,2048,512]{1,2,0:T(8,128)(2,1)}), bf16[8,2048,512]{1,2,0:T(8,128)(2,1)}, u32[]{:S(2)}, u32[]{:S(2)}) async-start(bf16[8,2048,512]{1,2,0:T(8,128)(2,1)} %stack.11), calls=%async_computation | async-start | bytes 33554432 | tf_op jit(solution)/shard_map/all_to_all | solution.py:66
  25.6 3.8 tile.4
  29.4 12.3 %copy.64 = bf16[16,8,128,256]{3,1,2,0:T(8,128)(2,1)} copy(bf16[16,8,128,256]{3,2,1,0:T(8,128)(2,1)} %bitcast.129) | data formatting | bytes 16777216
  41.7 7.3 %slice.290 = bf16[128,32640]{1,0:T(8,128)(2,1)} slice(bf16[128,32768]{1,0:T(8,128)(2,1)} %bitcast.130), slice={[0:128], [0:32640]} | slice | bytes 16711680 | tf_op jit(solution)/shard_map/slice | solution.py:18
  48.9 29.7 %reshape.195 = bf16[128,128,255]{2,1,0:T(8,128)(2,1)} reshape(bf16[128,32640]{1,0:T(8,128)(2,1)} %slice.290) | data formatting | bytes 16711680 | tf_op jit(solution)/shard_map/reshape | solution.py:18
  80.5 311.2 %all-to-all-done = bf16[8,2048,512]{1,2,0:T(8,128)(2,1)} async-done(((bf16[8,2048,512]{1,2,0:T(8,128)(2,1)}), bf16[8,2048,512]{1,2,0:T(8,128)(2,1)}, u32[]{:S(2)}, u32[]{:S(2)}) %all-to-all-start) | async-done | bytes 16777248 | tf_op jit(solution)/shard_map/all_to_all | solution.py:66
  391.7 8.4 %fusion.4 = bf16[128,2048]{1,0:T(8,128)(2,1)S(1)} fusion(bf16[2048,4096]{0,1:T(8,128)(2,1)} %bitcast.6, bf16[1,1,128,4096]{3,2,1,0:T(8,128)(2,1)} %all-gather.6.cloned.1.call-done, bf16[1,2,1,128,2048]{4,3,2,1,0:T(8,128)(2,1)S(1)} %copy-done.9), kind=kOutput, calls=%fused_computation.6 | convolution fusion | flops 2148270080 | bytes 18874368 | tf_op jit(solution)/shard_map/dot_general | solution.py:61
  402.1 1.7 fusion.20
  410.6 2.3 fusion.2
  414.2 2.5 fusion.9
  416.7 2.3 collective-permute-start
  421.7 6.1 reshape.201
  427.8 1.9 slice_reduce_fusion.15
  429.8 2.8 copy.66
  434.0 6.2 reshape.203
  440.2 1.9 slice_reduce_fusion.14
  442.2 2.8 copy.67
  446.5 6.2 reshape.205
  452.7 1.9 slice_reduce_fusion.13
  454.6 3.2 copy.68
  459.3 6.2 reshape.207
  465.5 1.9 slice_reduce_fusion.12
  467.4 2.8 copy.69
  471.7 6.1 reshape.209
  477.8 1.9 slice_reduce_fusion.11
  479.8 2.8 copy.70
  484.0 6.2 reshape.211
  490.2 1.9 slice_reduce_fusion.10
  495.8 2.8 copy.71
  500.0 6.1 reshape.213
  506.2 2.8 copy.72
  510.4 6.2 reshape.215
  517.9 2.0 slice_reduce_fusion.9
  520.0 1.9 slice_reduce_fusion.8
  523.0 8.4 %fusion.5 = bf16[128,2048]{1,0:T(8,128)(2,1)S(1)} fusion(bf16[128,4096]{1,0:T(8,128)(2,1)} %all-gather.4.cloned.1.call-done, bf16[2048,4096]{0,1:T(8,128)(2,1)} %bitcast.6, bf16[1,2,1,128,2048]{4,3,2,1,0:T(8,128)(2,1)} %param.7), kind=kOutput, calls=%fused_computation.7 | convolution fusion | flops 2148270080 | bytes 18874368 | tf_op jit(solution)/shard_map/dot_general | solution.py:61
  533.7 1.7 fusion.29
  537.1 1.9 fusion.31
  540.7 1.7 fusion.33
  542.8 3.3 fusion
  548.8 6.2 reshape.217
  554.9 1.9 slice_reduce_fusion.7
  556.9 2.8 copy.74
  561.2 6.1 reshape.219
  567.3 1.9 slice_reduce_fusion.6
  569.3 2.8 copy.75
  573.5 6.6 reshape.221
  580.1 1.9 slice_reduce_fusion.5
  582.1 2.8 copy.76
  586.4 6.2 reshape.223
  592.6 1.9 slice_reduce_fusion.4
  594.5 2.8 copy.77
  598.8 6.2 reshape.225
  605.0 1.9 slice_reduce_fusion.3
  606.9 2.8 copy.78
  611.2 6.3 reshape.227
  617.5 1.9 slice_reduce_fusion.2
  619.4 2.8 copy.79
  623.7 6.2 reshape.229
  629.8 1.9 slice_reduce_fusion.1
  633.2 4.6 reshape.231
  637.8 2.0 slice_reduce_fusion
  643.4 30.9 %reduce-scatter.4.cloned.1.call-done = f32[16,128]{1,0:T(8,128)} async-done(((f32[128,128]{1,0:T(8,128)}), f32[16,128]{1,0:T(8,128)}) %reduce-scatter.4.cloned.1.call-update) | async-done | bytes 8208
  (106 shorter events, 55.3 us)
Async XLA Ops:
  16.1 9.4 %copy-start.10 = (bf16[1,128,128]{2,1,0:T(8,128)(2,1)S(1)}, bf16[1,128,128]{2,1,0:T(8,128)(2,1)}, u32[]{:S(2)}) copy-start(bf16[1,128,128]{2,1,0:T(8,128)(2,1)} %param.11) | copy-start | bytes 98308
  16.1 375.6 %all-to-all-start = ((bf16[8,2048,512]{1,2,0:T(8,128)(2,1)}), bf16[8,2048,512]{1,2,0:T(8,128)(2,1)}, u32[]{:S(2)}, u32[]{:S(2)}) async-start(bf16[8,2048,512]{1,2,0:T(8,128)(2,1)} %stack.11), calls=%async_computation | async-start | bytes 33554432 | tf_op jit(solution)/shard_map/all_to_all | solution.py:66
  24.7 55.8 %all-gather.6.cloned.1.call-start = ((), (), s32[]{:S(2)}) async-start(), calls=%async_computation.3 | async-start | bytes 1572864 | tf_op jit(solution)/shard_map/all_gather | solution.py:58
  25.4 497.5 %all-gather.4.cloned.1.call-start = ((), (), s32[]{:S(2)}) async-start(), calls=%async_computation.2 | async-start | bytes 1572864 | tf_op jit(solution)/shard_map/all_gather | solution.py:58
  48.9 29.7 %copy-start.1 = (bf16[1,2,1,128,2048]{4,3,2,1,0:T(8,128)(2,1)S(1)}, bf16[1,2,1,128,2048]{4,3,2,1,0:T(8,128)(2,1)}, u32[]{:S(2)}) copy-start(bf16[1,2,1,128,2048]{4,3,2,1,0:T(8,128)(2,1)} %param.8) | copy-start | bytes 3145732
  48.9 29.7 %copy-start.8 = (bf16[1,2,1,128,2048]{4,3,2,1,0:T(8,128)(2,1)S(1)}, bf16[1,2,1,128,2048]{4,3,2,1,0:T(8,128)(2,1)}, u32[]{:S(2)}) copy-start(bf16[1,2,1,128,2048]{4,3,2,1,0:T(8,128)(2,1)} %param.6) | copy-start | bytes 3145732
  79.1 312.6 %copy-start.9 = (bf16[1,2,1,128,2048]{4,3,2,1,0:T(8,128)(2,1)S(1)}, bf16[1,2,1,128,2048]{4,3,2,1,0:T(8,128)(2,1)}, u32[]{:S(2)}) copy-start(bf16[1,2,1,128,2048]{4,3,2,1,0:T(8,128)(2,1)} %param.7) | copy-start | bytes 3145732
  400.4 10.1 %slice-start = ((s8[8388608]{0:T(1024)(128)(4,1)}), s8[4194304]{0:T(1024)(128)(4,1)S(1)}, s32[]{:S(2)}) async-start(s8[8388608]{0:T(1024)(128)(4,1)} %bitcast.125), calls=%async_computation.5 | async-start | bytes 8388608
  405.5 5.0 slice-start.1
  412.8 1.3 copy-start.4
  414.2 4.8 copy-start
  416.7 78.8 %collective-permute-start = (bf16[128,2048]{1,0:T(8,128)(2,1)}, bf16[128,2048]{1,0:T(8,128)(2,1)}, u32[]{:S(2)}, u32[]{:S(2)}) collective-permute-start(bf16[128,2048]{1,0:T(8,128)(2,1)} %fusion.9), channel_id=1, source_target_pairs={{16,0},{32,16},{48,32},{64,48},{80,64},{96,80},{112,96},{128,112},... | collective-permute-start | bytes 1572872 | tf_op jit(solution)/shard_map/ppermute | solution.py:11
  495.5 178.7 %reduce-scatter.4.cloned.1.call-start = ((), (), s32[]{:S(2)}) async-start(), calls=%async_computation.4 | async-start | bytes 73728
  516.6 5.3 copy-start.2
  517.9 4.0 copy-start.5
  533.7 9.1 %slice-start.2 = ((s8[8388608]{0:T(1024)(128)(4,1)}), s8[4194304]{0:T(1024)(128)(4,1)S(1)}, s32[]{:S(2)}) async-start(s8[8388608]{0:T(1024)(128)(4,1)} %bitcast.127), calls=%async_computation.7 | async-start | bytes 8388608
  539.1 3.7 slice-start.3
  633.2 7.5 %copy-start.6 = (f32[128,16,128]{2,1,0:T(8,128)S(1)}, f32[128,16,128]{2,1,0:T(8,128)}, u32[]{:S(2)}) copy-start(f32[128,16,128]{2,1,0:T(8,128)} %fusion) | copy-start | bytes 3145732
  637.8 3.2 copy-start.3
  641.0 1.3 copy-start.7
Sparse Core Ops, SparseCore 0:
  27.3 28.6 all-gather.5
  495.7 23.9 all-gather.3
  640.8 33.4 reduce-scatter.3
